TPU v7x, 256 devices: a whole 4x4x8 slice. The times are simulated.
256 devices in a mesh: lon: 16 (over z, core), lat: 16 (over x, y).
Axes of the slice: x: 4, y: 4, z: 8, core: 2. Of those that a mesh axis runs over, the one named last changes fastest.
Arguments:
- state: float32 [3, 16, 512, 4096], P(None, None, 'lat', 'lon'), may hold values from -6 to 6
- kmt: int32 [512, 4096], P('lat', 'lon'), may hold values from 0 to 16, as said below
- first_guess: float32 [512, 4096], P('lat', 'lon'), may hold values from -6 to 6
Outputs:
- next_state: float32 [3, 16, 512, 4096], P(None, None, 'lat', 'lon')
- pressure: float32 [512, 4096], P('lat', 'lon')
Inputs may be any that keep to these rules, and one draw needn't show every extreme that they name: `kmt`: 0 marks a land column.
All inputs are finite; a program needn't handle non-finite values.
Results may differ from a plain program's by a relative error of at most 0.0001.
Values sent between devices are 32-bit elements; how exact they have to be, the bound alone decides.
No kernel may reach another device: no remote copies, remote signals or barrier semaphores. Data moves between devices by JAX's collectives and lax.ppermute only.
A program may use at most 64 MiB of HBM per device.

v0:
```python
import jax
import jax.numpy as jnp
from jax import lax
from jax.sharding import PartitionSpec as P

ITERS = 4


viscosity = 0.12
diffusivity = 0.1
advection_scale = 0.5
vertical_mix = 0.2
coriolis_scale = 0.6
time_step = 0.5
storage = 0.5
gravity = 1.5
neighbours = (
    (0, 1, 2.0 / 3.0),
    (0, -1, 2.0 / 3.0),
    (1, 0, 2.0 / 3.0),
    (-1, 0, 2.0 / 3.0),
    (1, 1, 1.0 / 6.0),
    (1, -1, 1.0 / 6.0),
    (-1, 1, 1.0 / 6.0),
    (-1, -1, 1.0 / 6.0),
)


def with_halo(value, sides, width):
    for axis, dim in sides:
        peers, length = (lax.axis_size(axis), value.shape[dim])
        up = [(i, (i + 1) % peers) for i in range(peers)]
        down = [(j, i) for i, j in up]
        last = lax.slice_in_dim(value, length - width, length, axis=dim)
        first = lax.slice_in_dim(value, 0, width, axis=dim)
        before = lax.ppermute(last, axis, up)
        after = lax.ppermute(first, axis, down)
        value = jnp.concatenate([before, value, after], axis=dim)
    return value


def beside(padded, row_shift, col_shift):
    height = padded.shape[-2]
    breadth = padded.shape[-1]
    return padded[
        ..., 1 + row_shift : height - 1 + row_shift, 1 + col_shift : breadth - 1 + col_shift
    ]


def close_lat(padded, width):
    rows = lax.broadcasted_iota(jnp.int32, padded.shape, padded.ndim - 2)
    where_now = lax.axis_index("lat")
    last_tile = lax.axis_size("lat") - 1
    cut = (rows < width) & (where_now == 0) | (rows >= padded.shape[-2] - width) & (
        where_now == last_tile
    )
    return jnp.where(cut, jnp.zeros_like(padded), padded)


def coriolis_rows(first_row, count, total_rows):
    rows = (first_row + jnp.arange(count, dtype=jnp.int32)).astype(jnp.float32)
    angle = jnp.pi / 180.0 * (-80.0 + 160.0 * (rows + 0.5) / total_rows)
    return coriolis_scale * jnp.sin(angle)


def tendencies(padded_state, padded_wet, coriolis):
    centre = beside(padded_state, 0, 0)
    wet_centre = beside(padded_wet, 0, 0)
    wet_east = beside(padded_wet, 0, 1)
    wet_west = beside(padded_wet, 0, -1)
    wet_north = beside(padded_wet, 1, 0)
    wet_south = beside(padded_wet, -1, 0)
    east_vals = beside(padded_state, 0, 1) * wet_east
    west_vals = beside(padded_state, 0, -1) * wet_west
    north_vals = beside(padded_state, 1, 0) * wet_north
    south_vals = beside(padded_state, -1, 0) * wet_south
    laplace = (
        east_vals
        + west_vals
        + north_vals
        + south_vals
        - (wet_east + wet_west + wet_north + wet_south) * centre
    )
    grad_east = 0.5 * (east_vals - west_vals)
    grad_north = 0.5 * (north_vals - south_vals)
    zonal = centre[0]
    merid = centre[1]
    tracer = centre[2]
    carried = zonal * grad_east + merid * grad_north
    rotation = coriolis[:, None]
    zonal_tend = viscosity * laplace[0] + rotation * merid - advection_scale * carried[0]
    merid_tend = viscosity * laplace[1] - rotation * zonal - advection_scale * carried[1]
    level_zero = jnp.zeros_like(tracer[:1])
    tracer_above = jnp.concatenate([level_zero, tracer[:-1]], axis=0)
    tracer_below = jnp.concatenate([tracer[1:], level_zero], axis=0)
    wet_above = jnp.concatenate([level_zero, wet_centre[:-1]], axis=0)
    wet_below = jnp.concatenate([wet_centre[1:], level_zero], axis=0)
    vertical = wet_above * (tracer_above - tracer) + wet_below * (tracer_below - tracer)
    tracer_tend = diffusivity * laplace[2] - advection_scale * carried[2] + vertical_mix * vertical
    return jnp.stack([zonal_tend, merid_tend, tracer_tend]) * wet_centre


def couplings(padded_depth):
    centre = beside(padded_depth, 0, 0)
    terms = jnp.stack(
        [
            weight * jnp.minimum(centre, beside(padded_depth, row_shift, col_shift))
            for row_shift, col_shift, weight in neighbours
        ]
    )
    return (terms, storage + jnp.sum(terms, axis=0))


def operate(padded, terms, diagonal):
    total = diagonal * beside(padded, 0, 0)
    for number, (row_shift, col_shift, weight) in enumerate(neighbours):
        total = total - terms[number] * beside(padded, row_shift, col_shift)
    return total


def on_device(state, kmt, first_guess):
    levels = state.shape[1]
    rows_here = state.shape[2]
    total_rows = rows_here * lax.axis_size("lat")
    first_row = lax.axis_index("lat") * rows_here
    kmt_wide = close_lat(with_halo(kmt, (("lon", 1), ("lat", 0)), 2), 2)
    wet_wide = (jnp.arange(levels, dtype=jnp.int32)[:, None, None] < kmt_wide[None]).astype(
        jnp.float32
    )
    wet_one = wet_wide[:, 1:-1, 1:-1]
    wet_here = wet_wide[:, 2:-2, 2:-2]
    padded_state = with_halo(state, (("lon", 3), ("lat", 2)), 1)
    coriolis = coriolis_rows(first_row, rows_here, total_rows)
    tend = tendencies(padded_state, wet_one, coriolis)
    advanced = state + time_step * tend
    transports = jnp.sum(advanced[:2] * wet_here[None], axis=1)
    padded_flow = close_lat(with_halo(transports, (("lon", 2), ("lat", 1)), 1), 1)
    divergence = 0.5 * (beside(padded_flow[0], 0, 1) - beside(padded_flow[0], 0, -1)) + 0.5 * (
        beside(padded_flow[1], 1, 0) - beside(padded_flow[1], -1, 0)
    )
    kmt_one = kmt_wide[1:-1, 1:-1]
    depth_padded = kmt_one.astype(jnp.float32) / levels
    terms, diagonal = couplings(depth_padded)
    ocean = (kmt > 0).astype(jnp.float32)
    start = first_guess * ocean
    rhs = storage * ocean * (start - time_step * divergence)

    def apply_operator(field):
        padded = close_lat(with_halo(field, (("lon", 1), ("lat", 0)), 1), 1)
        return (operate(padded, terms, diagonal), padded)

    def precond_sum(residual, scaled):
        return lax.psum(jnp.sum(residual * scaled), ("lon", "lat"))

    iterate = start
    image, padded_iter = apply_operator(iterate)
    residual = rhs - image
    scaled = residual / diagonal
    direction = scaled
    norm_now = precond_sum(residual, scaled)
    for sweep in range(ITERS):
        image, padded_dir = apply_operator(direction)
        step_size = norm_now / lax.psum(jnp.sum(direction * image), ("lon", "lat"))
        iterate = iterate + step_size * direction
        padded_iter = padded_iter + step_size * padded_dir
        residual = residual - step_size * image
        if sweep + 1 < ITERS:
            scaled = residual / diagonal
            norm_next = precond_sum(residual, scaled)
            direction = scaled + norm_next / norm_now * direction
            norm_now = norm_next
    padded_height = close_lat(with_halo(iterate, (("lon", 1), ("lat", 0)), 1), 1)
    slope_east = 0.5 * (beside(padded_height, 0, 1) - beside(padded_height, 0, -1))
    slope_north = 0.5 * (beside(padded_height, 1, 0) - beside(padded_height, -1, 0))
    correction = jnp.stack([slope_east, slope_north, jnp.zeros_like(slope_east)]) * (
        time_step * gravity
    )
    next_state = (advanced - correction[:, None]) * wet_here[None]
    return (next_state, gravity * iterate)


def solution(mesh):
    placed = (P(None, None, "lat", "lon"), P("lat", "lon"), P("lat", "lon"))
    return jax.shard_map(
        on_device,
        mesh=mesh,
        in_specs=placed,
        out_specs=(P(None, None, "lat", "lon"), P("lat", "lon")),
        check_vma=False,
    )
```

profile of v0, /device:TPU:1, one launch (start us, length us, event | category | flops | bytes accessed | tf_op | source)
XLA Modules:
  0.0 667.3 jit_solution(15774962969407826093)
XLA Ops:
  1.5 3.2 collective-permute-start.13
  6.9 3.6 collective-permute-start
  10.5 2.8 collective-permute-start.2
  17.2 5.0 collective-permute-start.4
  22.9 4.8 collective-permute-start.15
  28.1 2.3 fusion.95
  30.8 2.0 copy.8
  34.5 4.8 collective-permute-start.6
  41.1 2.3 multiply_subtract_fusion
  43.4 2.3 multiply_add_fusion
  48.5 3.2 collective-permute-start.9
  53.0 5.3 collective-permute-start.11
  59.1 5.0 collective-permute-done.10
  64.5 4.8 collective-permute-start.17
  73.3 3.1 collective-permute-done.18
  78.0 74.8 %all-reduce.4 = (f32[]{:T(128)}, f32[]{:T(128)}) all-reduce(f32[]{:T(128)} %get-tuple-element.3, f32[]{:T(128)} %get-tuple-element.2), channel_id=1, replica_groups=mesh['lon'=16,'lat'=16] {'lon','lat'}, use_global_device_ids=true, to_apply=%region_2.3 | all-reduce | flops 2 | bytes 16 | tf_op jit(solution)/shard_map/psum | solution.py:153
  154.1 2.0 multiply_reduce_fusion.4
  156.1 74.5 %psum.58 = f32[]{:T(128)} all-reduce(f32[]{:T(128)} %get-tuple-element.15), channel_id=1, replica_groups=mesh['lon'=16,'lat'=16] {'lon','lat'}, use_global_device_ids=true, to_apply=%region_6.7 | all-reduce | flops 1 | bytes 8 | tf_op jit(solution)/shard_map/psum | solution.py:153
  236.0 1.8 collective-permute-start.23
  238.6 5.0 collective-permute-done.22
  245.1 74.6 %psum.59 = f32[]{:T(128)} all-reduce(f32[]{:T(128)} %get-tuple-element.13), channel_id=1, replica_groups=mesh['lon'=16,'lat'=16] {'lon','lat'}, use_global_device_ids=true, to_apply=%region_8.9 | all-reduce | flops 1 | bytes 8 | tf_op jit(solution)/shard_map/psum | solution.py:163
  321.1 2.0 multiply_reduce_fusion.2
  323.1 74.2 %psum.60 = f32[]{:T(128)} all-reduce(f32[]{:T(128)} %get-tuple-element.10), channel_id=1, replica_groups=mesh['lon'=16,'lat'=16] {'lon','lat'}, use_global_device_ids=true, to_apply=%region_10.11 | all-reduce | flops 1 | bytes 8 | tf_op jit(solution)/shard_map/psum | solution.py:153
  402.8 1.8 collective-permute-start.27
  405.4 5.0 collective-permute-done.26
  412.0 74.6 %psum.61 = f32[]{:T(128)} all-reduce(f32[]{:T(128)} %get-tuple-element.8), channel_id=1, replica_groups=mesh['lon'=16,'lat'=16] {'lon','lat'}, use_global_device_ids=true, to_apply=%region_12.13 | all-reduce | flops 1 | bytes 8 | tf_op jit(solution)/shard_map/psum | solution.py:163
  488.6 74.2 %psum.62 = f32[]{:T(128)} all-reduce(f32[]{:T(128)} %multiply_reduce_fusion), channel_id=1, replica_groups=mesh['lon'=16,'lat'=16] {'lon','lat'}, use_global_device_ids=true, to_apply=%region_14.15 | all-reduce | flops 1 | bytes 8 | tf_op jit(solution)/shard_map/psum | solution.py:153
  567.5 2.0 collective-permute-start.31
  570.3 5.0 collective-permute-done.30
  576.9 74.6 %psum.63 = f32[]{:T(128)} all-reduce(f32[]{:T(128)} %fusion.27), channel_id=1, replica_groups=mesh['lon'=16,'lat'=16] {'lon','lat'}, use_global_device_ids=true, to_apply=%region_16.17 | all-reduce | flops 1 | bytes 8 | tf_op jit(solution)/shard_map/psum | solution.py:163
  659.8 4.5 collective-permute-done.34
  664.7 2.6 subtract_multiply_fusion
  (146 shorter events, 48.9 us)
Async XLA Ops:
  1.5 20.7 %collective-permute-start.13 = (f32[32,1]{1,0:T(8,128)S(1)}, f32[32,1]{1,0:T(8,128)S(1)}, u32[]{:S(2)}, u32[]{:S(2)}) collective-permute-start(f32[32,1]{1,0:T(8,128)S(1)} %get-tuple-element.83), channel_id=1, source_target_pairs={{16,0},{32,16},{48,32},{64,48},{80,64},{96,80},{112,96},{128,112},... | collective-permute-start | bytes 392 | tf_op jit(solution)/shard_map/ppermute | solution.py:37
  4.7 17.4 %collective-permute-start.12 = (f32[32,1]{1,0:T(8,128)S(1)}, f32[32,1]{1,0:T(8,128)S(1)}, u32[]{:S(2)}, u32[]{:S(2)}) collective-permute-start(f32[32,1]{1,0:T(8,128)S(1)} %get-tuple-element.82), channel_id=1, source_target_pairs={{0,16},{16,32},{32,48},{48,64},{64,80},{80,96},{96,112},{112,128},... | collective-permute-start | bytes 392 | tf_op jit(solution)/shard_map/ppermute | solution.py:36
  6.9 23.6 %collective-permute-start = (f32[3,16,32,1]{2,1,3,0:T(8,128)S(1)}, f32[3,16,32,1]{2,1,3,0:T(8,128)S(1)}, u32[]{:S(2)}, u32[]{:S(2)}) collective-permute-start(f32[3,16,32,1]{2,1,3,0:T(8,128)S(1)} %copy.11), channel_id=1, source_target_pairs={{16,0},{32,16},{48,32},{64,48},{80,64},{96,80},{112,96},{128,112},... | collective-permute-start | bytes 18440 | tf_op jit(solution)/shard_map/ppermute | solution.py:37
  10.5 6.6 collective-permute-start.2
  13.4 3.8 collective-permute-start.1
  17.1 13.7 %collective-permute-start.5 = (f32[3,16,32,1]{2,1,3,0:T(8,128)}, f32[3,16,32,1]{2,1,3,0:T(8,128)}, u32[]{:S(2)}, u32[]{:S(2)}) collective-permute-start(f32[3,16,32,1]{2,1,3,0:T(8,128)} %copy.12), channel_id=1, source_target_pairs={{0,16},{16,32},{32,48},{48,64},{64,80},{80,96},{96,112},{112,128},... | collective-permute-start | bytes 18440 | tf_op jit(solution)/shard_map/ppermute | solution.py:36
  17.2 10.4 %collective-permute-start.4 = (s32[2,260]{1,0:T(2,128)S(1)}, s32[2,260]{1,0:T(2,128)S(1)}, u32[]{:S(2)}, u32[]{:S(2)}) collective-permute-start(s32[2,260]{1,0:T(2,128)S(1)} %get-tuple-element.69), channel_id=1, source_target_pairs={{1,0},{2,1},{3,2},{4,3},{5,4},{6,5},{7,6},{8,7},{9,8},{10,9},{11,1... | collective-permute-start | bytes 6248 | tf_op jit(solution)/shard_map/ppermute | solution.py:37
  22.2 5.8 collective-permute-start.3
  22.9 28.9 %collective-permute-start.15 = (f32[1,258]{1,0:T(1,128)}, f32[1,258]{1,0:T(1,128)S(1)}, u32[]{:S(2)}, u32[]{:S(2)}) collective-permute-start(f32[1,258]{1,0:T(1,128)} %get-tuple-element.67), channel_id=1, source_target_pairs={{1,0},{2,1},{3,2},{4,3},{5,4},{6,5},{7,6},{8,7},{9,8},{10,9},{11,1... | collective-permute-start | bytes 3104 | tf_op jit(solution)/shard_map/ppermute | solution.py:37
  27.6 24.1 %collective-permute-start.14 = (f32[1,258]{1,0:T(1,128)}, f32[1,258]{1,0:T(1,128)}, u32[]{:S(2)}, u32[]{:S(2)}) collective-permute-start(f32[1,258]{1,0:T(1,128)} %get-tuple-element.66), channel_id=1, source_target_pairs={{0,1},{1,2},{2,3},{3,4},{4,5},{5,6},{6,7},{7,8},{8,9},{9,10},{10,1... | collective-permute-start | bytes 3104 | tf_op jit(solution)/shard_map/ppermute | solution.py:36
  34.5 6.6 collective-permute-start.7
  34.5 6.5 collective-permute-start.6
  48.5 4.0 collective-permute-start.9
  53.0 6.1 collective-permute-start.11
  58.3 5.8 collective-permute-start.10
  64.5 5.6 collective-permute-start.17
  70.6 2.7 collective-permute-start.19
  70.6 5.8 collective-permute-start.18
  232.8 3.2 collective-permute-start.21
  233.5 2.5 collective-permute-start.20
  236.0 2.6 collective-permute-start.23
  237.9 5.8 collective-permute-start.22
  399.6 3.2 collective-permute-start.25
  402.8 2.6 collective-permute-start.27
  404.6 5.8 collective-permute-start.26
  564.2 3.2 collective-permute-start.29
  564.9 2.5 collective-permute-start.28
  567.5 2.8 collective-permute-start.31
  569.5 5.8 collective-permute-start.30
  653.6 3.7 collective-permute-start.33
  654.2 3.1 collective-permute-start.32
  658.6 5.8 collective-permute-start.34
  (22 other events, 1014.4 us)
where the time goes:
time: 671 us; the launch traced here: 667 us
  blocking collectives  522 us (78%)
  starting transfers between devices  53.8 us (8%)
  waiting for transfers between devices  41.7 us (6%)
  other arithmetic  30.7 us (5%)
  between operations  10.5 us (2%)
  local copies, waits for them, and re-layouts  9.06 us (1%)
    psum x4, blocking collectives, precond_sum(): return lax.psum(jnp.sum(residual * scaled), ('lon', 'lat'))  298 us
    psum x3, blocking collectives, on_device(): step_size = norm_now / lax.psum(jnp.sum(direction * image), ('lon', 'lat'))  224 us
    ppermute x18, starting transfers between devices, with_halo(): after = lax.ppermute(first, axis, down)  47 us
    ppermute x18, waiting for transfers between devices, with_halo(): before = lax.ppermute(last, axis, up)  30.2 us
  transfers between devices with their start and end apart: 36, of which 22 were waited for; matrix products, arithmetic and copies ran while one was open for 3% of the time, Pallas kernels for 0%

commit v1 on v0

v1 whole, which is shorter than its diff:
```python
import functools

import jax
import jax.numpy as jnp
from jax import lax
from jax.experimental import pallas as pl
from jax.experimental.pallas import tpu as pltpu
from jax.sharding import PartitionSpec as P

ITERS = 4
F32 = jnp.float32

viscosity = 0.12
diffusivity = 0.1
advection_scale = 0.5
vertical_mix = 0.2
coriolis_scale = 0.6
time_step = 0.5
storage = 0.5
gravity = 1.5
edge_weight = 2.0 / 3.0
corner_weight = 1.0 / 6.0

TILE = 8
LANES = 128
HALO = 6

LOWEST = storage / (storage + 4 * edge_weight + 4 * corner_weight)
HIGHEST = 2.0 - LOWEST
VMEM_LIMIT = 48 * 1024 * 1024


def params():
    return pltpu.CompilerParams(vmem_limit_bytes=VMEM_LIMIT)


def turn(x, shift, axis):
    return pltpu.roll(x, shift % x.shape[axis], axis)


def east_of(x):
    return turn(x, -1, 1)


def west_of(x):
    return turn(x, 1, 1)


def north_of(x):
    return turn(x, -1, 0)


def south_of(x):
    return turn(x, 1, 0)


def lane_of(shape):
    return lax.broadcasted_iota(jnp.int32, shape, len(shape) - 1)


def is_even(axis):
    return lax.rem(lax.axis_index(axis), 2) == 0


def swap(first, a, b):
    return jnp.where(first, a, b), jnp.where(first, b, a)


def pack_rows(
    low, high, kmt_low, kmt_high, guess_low, guess_high, msg_even, msg_odd
):
    levels = low.shape[1]
    even = is_even("lat")
    row = lax.broadcasted_iota(jnp.int32, low.shape[2:], 0)

    def put(slot, to_north, to_south):
        a, b = swap(even, to_north, to_south)
        msg_even[slot] = a
        msg_odd[slot] = b

    for k in range(levels):
        north = jnp.where(row == 0, turn(high[2, k], 1, 0), high[0, k])
        south = jnp.where(row == TILE - 1, turn(low[2, k], -1, 0), low[0, k])
        put(k, north, south)
        put(levels + k, high[1, k], low[1, k])
    put(2 * levels, kmt_high[...].astype(F32), kmt_low[...].astype(F32))
    put(2 * levels + 1, guess_high[...], guess_low[...])


def stacked(south, own, north):
    return jnp.concatenate([south, own, north], axis=0)


def pack_cols(first, last, kmt, guess, rows_even, rows_odd, msg_even, msg_odd):
    levels = first.shape[1]
    tall = first.shape[2] + 2 * TILE
    lat_even = is_even("lat")
    lon_even = is_even("lon")
    group = lane_of((tall, LANES)) // TILE
    breadth = kmt.shape[1]

    def halos(slot, cols):
        north, south = swap(lat_even, rows_even[slot, :, cols], rows_odd[slot, :, cols])
        return south, north

    west_cols = slice(0, LANES)
    east_cols = slice(breadth - LANES, breadth)

    def columns(field, k):
        out = []
        for edge, cols in ((first, west_cols), (last, east_cols)):
            own = edge[field, k]
            south, north = halos(k if field != 1 else levels + k, cols)
            if field == 2:
                south, north = (turn(south, -1, 0), turn(north, 1, 0))
            out.append(stacked(south, own, north))
        return out

    def place(k, west, east, acc):
        to_west, to_east = acc
        to_west = jnp.where(group == k, pltpu.roll(west, 2 + TILE * k, 1), to_west)
        to_east = jnp.where(
            group == k, pltpu.roll(east, lax.rem(HALO + TILE * k, LANES), 1), to_east
        )
        return to_west, to_east

    def put(slot, acc):
        to_west, to_east = acc
        a, b = swap(lon_even, to_east, to_west)
        msg_even[slot] = a
        msg_odd[slot] = b

    blank = (jnp.zeros((tall, LANES), F32),) * 2
    for field in range(3):

        def body(k, acc, field=field):
            west, east = columns(field, k)
            return place(k, west, east, acc)

        put(field, lax.fori_loop(0, levels, body, blank, unroll=4))
    acc = blank
    for number, own in enumerate((kmt[...].astype(F32), guess[...])):
        sides = []
        for cols in (west_cols, east_cols):
            south, north = halos(2 * levels + number, cols)
            sides.append(stacked(south, own[:, cols], north))
        acc = place(jnp.int32(number), sides[0], sides[1], acc)
    put(3, acc)


def rotation_rows(tall, lanes, rows_here):
    total_rows = rows_here * lax.axis_size("lat")
    row = lax.broadcasted_iota(jnp.int32, (tall, lanes), 0)
    row = (row - TILE + lax.axis_index("lat") * rows_here).astype(F32)
    angle = jnp.pi / 180.0 * (-80.0 + 160.0 * (row + 0.5) / total_rows)
    return coriolis_scale * jnp.sin(angle)


def around(x):
    return east_of(x), west_of(x), north_of(x), south_of(x)


def count_wet(sides, level):
    total = None
    for side in sides:
        term = jnp.where(side > level, 1.0, 0.0)
        total = term if total is None else total + term
    return total


def spread(x, sides, count, coefficient, zonal, merid):
    east, west, north, south = sides
    laplace = east + west + north + south - count * x
    return (
        (time_step * coefficient) * laplace
        - zonal * (east - west)
        - merid * (north - south)
    )


carry = 0.5 * time_step * advection_scale


def advance_flow(u, v, wet, count, half_turn):
    zonal, merid = (carry * u, carry * v)
    new_u = u + (spread(u, around(u), count, viscosity, zonal, merid) + half_turn * v)
    new_v = v + (spread(v, around(v), count, viscosity, zonal, merid) - half_turn * u)
    return jnp.where(wet, new_u, 0.0), jnp.where(wet, new_v, 0.0)


def advance_inner(state, kmt, rows_even, rows_odd, out, flow_u, flow_v, turning):
    levels, rows_here, breadth = state.shape[1:]
    tall = rows_here + 2 * TILE
    lat_even = is_even("lat")

    def halos(slot):
        north, south = swap(lat_even, rows_even[slot], rows_odd[slot])
        return south, north

    south, north = halos(2 * levels)
    depth = stacked(south, kmt[...].astype(F32), north)
    beside = around(depth)
    rotation = rotation_rows(tall, LANES, rows_here)
    turning[...] = rotation
    half_turn = time_step * rotation[:, :1]
    own = slice(TILE, TILE + rows_here)
    flow_u[...] = jnp.zeros_like(flow_u)
    flow_v[...] = jnp.zeros_like(flow_v)

    def body(k, _):
        level = k.astype(F32)
        wet = depth > level
        count = count_wet(beside, level)
        u_south, u_north = halos(k)
        v_south, v_north = halos(levels + k)
        u = jnp.where(wet, stacked(u_south, state[0, k], u_north), 0.0)
        v = jnp.where(wet, stacked(v_south, state[1, k], v_north), 0.0)
        new_u, new_v = advance_flow(u, v, wet, count, half_turn)
        flow_u[...] += new_u
        flow_v[...] += new_v
        out[0, k] = new_u[own]
        out[1, k] = new_v[own]
        here = state[2, k]
        tracer = jnp.where(
            wet, stacked(turn(u_south, -1, 0), here, turn(u_north, 1, 0)), 0.0
        )
        east, west = (east_of(tracer[own]), west_of(tracer[own]))
        north, south = (north_of(tracer)[own], south_of(tracer)[own])
        change = spread(
            tracer[own],
            (east, west, north, south),
            count[own],
            diffusivity,
            carry * u[own],
            carry * v[own],
        )
        above = state[2, jnp.maximum(k - 1, 0)]
        below = state[2, jnp.minimum(k + 1, levels - 1)]
        vertical = (above - here) + jnp.where(depth[own] > level + 1.0, below - here, 0.0)
        out[2, k] = jnp.where(
            wet[own], here + (change + (time_step * vertical_mix) * vertical), 0.0
        )
        return 0

    lax.fori_loop(0, levels, body, 0)


def over_groups(x):
    for step in (TILE, 2 * TILE, 4 * TILE, 8 * TILE):
        x = x + pltpu.roll(x, step, 1)
    return x


def krylov(
    sent_even, sent_odd, got_even, got_odd, flow_u, flow_v, kmt, guess,
    rows_even, rows_odd, turning, edges, basis, moments,
):
    levels = (rows_even.shape[0] - 2) // 2
    rows_here, breadth = kmt.shape
    tall = rows_here + 2 * TILE
    lat_even = is_even("lat")
    lon_even = is_even("lon")
    lane = lane_of((tall, LANES))
    place = lax.rem(lane, TILE)
    group = lane // TILE
    level = group.astype(F32)
    own = slice(TILE, TILE + rows_here)
    half_turn = time_step * turning[...]

    def strips(slot):
        to_east, to_west = swap(lon_even, sent_even[slot], sent_odd[slot])
        from_east, from_west = swap(lon_even, got_even[slot], got_odd[slot])
        west = jnp.where(place < HALO, from_west, turn(to_west, 4, 1))
        east = jnp.where(place >= TILE - HALO, from_east, turn(to_east, -4, 1))
        return west, east

    u_sides, v_sides, t_sides, other = [strips(slot) for slot in range(4)]
    sums = []
    for side in range(2):
        depth = over_groups(jnp.where(group == 0, other[side], 0.0))
        start = over_groups(jnp.where(group == 1, other[side], 0.0))
        wet = depth > level
        count = count_wet(around(depth), level)
        u = jnp.where(wet, u_sides[side], 0.0)
        v = jnp.where(wet, v_sides[side], 0.0)
        new_u, new_v = advance_flow(u, v, wet, count, half_turn)
        here = jnp.where(wet, t_sides[side], 0.0)
        change = spread(here, around(here), count, diffusivity, carry * u, carry * v)
        above = jnp.where(group > 0, turn(here, TILE, 1) - here, 0.0)
        below = jnp.where(depth > level + 1.0, turn(here, -TILE, 1) - here, 0.0)
        new_t = jnp.where(
            wet, here + (change + (time_step * vertical_mix) * (above + below)), 0.0
        )
        edges[side, 0] = new_u[own]
        edges[side, 1] = new_v[own]
        edges[side, 2] = new_t[own]
        sums.append((over_groups(new_u), over_groups(new_v), depth, start))

    def assemble(field, number, seam):
        west = turn(sums[0][number], 2, 1)
        east = turn(sums[1][number], -2, 1)
        halo = jnp.where(lane < LANES // 2, east, west)
        tiles = [field[:, i : i + LANES] for i in range(0, breadth, LANES)]
        if seam:
            tiles[0] = jnp.where(lane == 0, west, tiles[0])
            tiles[-1] = jnp.where(lane == LANES - 1, east, tiles[-1])
        return jnp.concatenate(tiles + [halo], axis=1)

    def tall_field(slot, value):
        north, south = swap(lat_even, rows_even[slot], rows_odd[slot])
        return stacked(south, value, north)

    wide_u = assemble(flow_u[...], 0, True)
    wide_v = assemble(flow_v[...], 1, True)
    wet_levels = assemble(tall_field(2 * levels, kmt[...].astype(F32)), 2, False)
    first = assemble(tall_field(2 * levels + 1, guess[...]), 3, False)

    divergence = 0.5 * (east_of(wide_u) - west_of(wide_u)) + 0.5 * (
        north_of(wide_v) - south_of(wide_v)
    )
    depth = wet_levels * (1.0 / levels)
    ocean = wet_levels > 0.0
    to_east = edge_weight * jnp.minimum(depth, east_of(depth))
    to_north = edge_weight * jnp.minimum(depth, north_of(depth))
    depth_north = north_of(depth)
    to_ne = corner_weight * jnp.minimum(depth, east_of(depth_north))
    to_nw = corner_weight * jnp.minimum(depth, west_of(depth_north))
    to_west = west_of(to_east)
    to_south = south_of(to_north)
    to_sw = south_of(west_of(to_ne))
    to_se = south_of(east_of(to_nw))
    diagonal = storage + (
        (to_east + to_west) + (to_north + to_south) + ((to_ne + to_nw) + (to_se + to_sw))
    )

    def neighbours(x):
        up, down = (north_of(x), south_of(x))
        eastern = to_east * x + to_ne_w * up + to_se_w * down
        western = to_west * x + to_nw_e * up + to_sw_e * down
        return to_north * up + to_south * down + (east_of(eastern) + west_of(western))

    to_ne_w = west_of(to_ne)
    to_se_w = west_of(to_se)
    to_nw_e = east_of(to_nw)
    to_sw_e = east_of(to_sw)
    to_east, to_west = (west_of(to_east), east_of(to_west))

    start = jnp.where(ocean, first, 0.0)
    rhs = jnp.where(ocean, storage * (start - time_step * divergence), 0.0)
    residual = rhs - (diagonal * start - neighbours(start))
    inverse = 1.0 / diagonal
    vectors = [residual * inverse]
    basis[0] = start
    basis[1] = vectors[0]
    for k in range(1, ITERS):
        vectors.append(neighbours(vectors[-1]) * inverse)
        basis[k + 1] = vectors[k]
    last = neighbours(vectors[-1])

    def inner(x):
        return x[own, :breadth]

    weighted = [inner(diagonal * x) for x in vectors] + [inner(last)]
    held = [inner(x) for x in vectors]
    slot = lane_of((1, LANES))
    total = jnp.zeros((1, LANES), F32)
    for m in range(2 * ITERS):
        product = held[m // 2] * weighted[(m + 1) // 2]
        total = jnp.where(slot == m, jnp.sum(product), total)
    moments[...] = total


def finish(shares, basis, edges, kmt, advanced, out, pressure):
    levels, rows_here, breadth = advanced.shape[1:]
    own = slice(TILE, TILE + rows_here)
    sums = jnp.sum(shares[...], axis=0, keepdims=True)
    size = 2 * ITERS
    res = [sums[:, m : m + 1] for m in range(size)]
    dirn = list(res)
    one, zero = (jnp.ones((1, 1), F32), jnp.zeros((1, 1), F32))
    res_in = [one] + [zero] * (ITERS - 1)
    dir_in = list(res_in)
    height_in = [zero] * ITERS
    for k in range(ITERS):
        step = res[k] / (dirn[k] - dirn[k + 1])
        step = jnp.clip(step, 1.0 / HIGHEST, 1.0 / LOWEST)
        height_in = [h + step * d for h, d in zip(height_in, dir_in)]
        if k + 1 < ITERS:
            new = [res[m] - step * (dirn[m] - dirn[m + 1]) for m in range(len(dirn) - 1)]
            ratio = jnp.clip(step * new[k + 1] / res[k], 0.0, HIGHEST / LOWEST)
            dirn = [n + ratio * d for n, d in zip(new, dirn)]
            res = new
            moved = [zero] + dir_in[:-1]
            res_in = [r - step * (d - m) for r, d, m in zip(res_in, dir_in, moved)]
            dir_in = [r + ratio * d for r, d in zip(res_in, dir_in)]
    height = basis[0]
    for k in range(ITERS):
        height = height + height_in[k] * basis[k + 1]
    pressure[...] = gravity * height[own, :breadth]
    pull = 0.5 * time_step * gravity
    slope_east = pull * (east_of(height) - west_of(height))[own, :breadth]
    slope_north = pull * (north_of(height) - south_of(height))[own, :breadth]
    wet_levels = kmt[...]
    lane = lane_of((rows_here, LANES))

    def body(k, _):
        wet = wet_levels > k
        for field, slope in ((0, slope_east), (1, slope_north), (2, None)):
            value = advanced[field, k]
            west = pltpu.roll(edges[0, field], lax.rem(2 * LANES - HALO - TILE * k, LANES), 1)
            east = pltpu.roll(
                edges[1, field], lax.rem(2 * LANES - 2 - TILE * k, LANES), 1
            )
            tiles = [value[:, i : i + LANES] for i in range(0, breadth, LANES)]
            tiles[0] = jnp.where(lane == 0, west, tiles[0])
            tiles[-1] = jnp.where(lane == LANES - 1, east, tiles[-1])
            value = jnp.concatenate(tiles, axis=1)
            if slope is not None:
                value = jnp.where(wet, value - slope, 0.0)
            out[field, k] = value
        return 0

    lax.fori_loop(0, levels, body, 0, unroll=2)


def pairs(axis):
    peers = lax.axis_size(axis)
    even = [(i, i ^ 1) for i in range(peers)]
    odd = [(i, ((i + 1) ^ 1) - 1) for i in range(1, peers - 1)]
    if axis == "lon":
        odd += [(0, peers - 1), (peers - 1, 0)]
    return even, odd


def exchange(axis, to_even, to_odd):
    even, odd = pairs(axis)
    return lax.ppermute(to_even, axis, even), lax.ppermute(to_odd, axis, odd)


def on_device(state, kmt, first_guess):
    _, levels, rows_here, breadth = state.shape
    tall = rows_here + 2 * TILE
    wide = breadth + LANES
    shape = lambda *dims: jax.ShapeDtypeStruct(dims, F32)

    last_row = rows_here // TILE - 1
    edge = lambda row: pl.BlockSpec((3, levels, TILE, breadth), lambda i: (0, 0, row, 0))
    flat = lambda row: pl.BlockSpec((TILE, breadth), lambda i: (row, 0))
    slots = 2 * levels + 2
    whole = lambda *dims: pl.BlockSpec(dims, lambda i: (0,) * len(dims))
    to_even, to_odd = pl.pallas_call(
        pack_rows,
        grid=(1,),
        in_specs=[edge(0), edge(last_row)] + [flat(0), flat(last_row)] * 2,
        out_specs=[whole(slots, TILE, breadth)] * 2,
        out_shape=[shape(slots, TILE, breadth)] * 2,
        compiler_params=params(),
    )(state, state, kmt, kmt, first_guess, first_guess)
    rows_even, rows_odd = exchange("lat", to_even, to_odd)

    last_lane = breadth // LANES - 1
    edge_cols = lambda col: pl.BlockSpec((3, levels, rows_here, LANES), lambda i: (0, 0, 0, col))
    rows_spec = whole(slots, TILE, breadth)
    field_spec = whole(rows_here, breadth)
    sent_even, sent_odd = pl.pallas_call(
        pack_cols,
        grid=(1,),
        in_specs=[edge_cols(0), edge_cols(last_lane), field_spec, field_spec, rows_spec, rows_spec],
        out_specs=[whole(4, tall, LANES)] * 2,
        out_shape=[shape(4, tall, LANES)] * 2,
        compiler_params=params(),
    )(state, state, kmt, first_guess, rows_even, rows_odd)
    got_even, got_odd = exchange("lon", sent_even, sent_odd)

    advanced, flow_u, flow_v, turning = pl.pallas_call(
        advance_inner,
        out_shape=[
            shape(3, levels, rows_here, breadth),
            shape(tall, breadth),
            shape(tall, breadth),
            shape(tall, LANES),
        ],
        compiler_params=params(),
        cost_estimate=pl.CostEstimate(
            flops=60 * state.size, bytes_accessed=8 * state.size, transcendentals=0
        ),
    )(state, kmt, rows_even, rows_odd)

    edges, basis, moments = pl.pallas_call(
        krylov,
        out_shape=[
            shape(2, 3, rows_here, LANES),
            shape(ITERS + 1, tall, wide),
            shape(1, LANES),
        ],
        compiler_params=params(),
    )(
        sent_even, sent_odd, got_even, got_odd, flow_u, flow_v, kmt, first_guess,
        rows_even, rows_odd, turning,
    )

    devices = lax.axis_size("lon") * lax.axis_size("lat")
    shares = jnp.broadcast_to(moments[None], (devices, 1, LANES))
    shares = lax.all_to_all(shares, ("lon", "lat"), 0, 0)
    next_state, pressure = pl.pallas_call(
        finish,
        out_shape=[shape(3, levels, rows_here, breadth), shape(rows_here, breadth)],
        compiler_params=params(),
    )(shares.reshape(devices, LANES), basis, edges, kmt, advanced)
    return next_state, pressure


def solution(mesh):
    placed = (P(None, None, "lat", "lon"), P("lat", "lon"), P("lat", "lon"))
    return jax.shard_map(
        on_device,
        mesh=mesh,
        in_specs=placed,
        out_specs=(P(None, None, "lat", "lon"), P("lat", "lon")),
        check_vma=False,
    )
```

time: 671 us -> 57.6 us (0.09)
  blocking collectives: 522 us -> 31.9 us
  starting transfers between devices: 53.8 us -> 7.23 us
  waiting for transfers between devices: 41.7 us -> 4.47 us
  other arithmetic: 30.7 us -> 0 us
  Pallas kernels: 0 us -> 9.97 us
  between operations: 10.5 us -> 0.73 us
    psum x7 -> x0, blocking collectives: 522 us -> none  [the longest x4 298 us: precond_sum(): return lax.psum(jnp.sum(residual * scaled), ('lon', 'lat'))]
    ppermute x36 -> x4, starting transfers between devices: 53.8 us -> 7.23 us  [exchange(): return (lax.ppermute(to_even, axis, even), lax.ppermute(to_odd, axis, odd))]
    ppermute x36 -> x4, waiting for transfers between devices: 41.7 us -> 4.47 us  [exchange(): return (lax.ppermute(to_even, axis, even), lax.ppermute(to_odd, axis, odd))]
    all_to_all x0 -> x1, blocking collectives: none -> 31.9 us  [on_device(): shares = lax.all_to_all(shares, ('lon', 'lat'), 0, 0)]
    reduce_sum x8 -> x0, other arithmetic: 10.7 us -> none  [the longest x4 5.85 us: on_device(): step_size = norm_now / lax.psum(jnp.sum(direction * image), ('lon', 'lat'))]
    pallas_call x0 -> x5, Pallas kernels: none -> 9.97 us  [the longest x1 3.48 us: on_device(): pl.pallas_call(finish, out_shape=[shape(3, levels, rows_here, breadth), s...]
  transfers between devices with their start and end apart: 36 -> 4, of which waited for: 22 -> 1; matrix products, arithmetic and copies ran while one was open for 3% -> 0% of each run, Pallas kernels for 0% -> 5%
where the time goes in v1:
time: 57.6 us; the launch traced here: 57.3 us
  blocking collectives  31.9 us (55%)
  Pallas kernels  9.97 us (17%)
  starting transfers between devices  7.23 us (13%)
  waiting for transfers between devices  4.47 us (8%)
  local copies, waits for them, and re-layouts  3 us (5%)
  between operations  0.73 us (1%)
    all_to_all x1, blocking collectives, on_device(): shares = lax.all_to_all(shares, ('lon', 'lat'), 0, 0)  31.9 us
    ppermute x4, starting transfers between devices, exchange(): return (lax.ppermute(to_even, axis, even), lax.ppermute(to_odd, axis, odd))  7.23 us
    ppermute x4, waiting for transfers between devices, exchange(): return (lax.ppermute(to_even, axis, even), lax.ppermute(to_odd, axis, odd))  4.47 us
    pallas_call x1, Pallas kernels, on_device(): pl.pallas_call(finish, out_shape=[shape(3, levels, rows_here, breadth), s...  3.48 us
    pallas_call x1, Pallas kernels, on_device(): pl.pallas_call(advance_inner, out_shape=[shape(3, levels, rows_here, brea...  3.06 us
    unnamed x10, local copies, waits for them, and re-layouts  2.93 us
    pallas_call x1, Pallas kernels, on_device(): pl.pallas_call(krylov, out_shape=[shape(2, 3, rows_here, LANES), shape(IT...  1.73 us
    pallas_call x1, Pallas kernels, on_device(): pl.pallas_call(pack_cols, grid=(1,), in_specs=[edge_cols(0), edge_cols(la...  1.64 us
  transfers between devices with their start and end apart: 4, of which 1 were waited for; matrix products, arithmetic and copies ran while one was open for 0% of the time, Pallas kernels for 5%

profile of v1, /device:TPU:1, one launch (start us, length us, event | category | flops | bytes accessed | tf_op | source)
XLA Modules:
  0.0 57.3 jit_solution(1972907140936273646)
XLA Ops:
  0.6 0.0 copy-start
  0.6 1.4 %copy-done = f32[3,16,32,256]{3,2,1,0:T(8,128)S(1)} copy-done((f32[3,16,32,256]{3,2,1,0:T(8,128)S(1)}, f32[3,16,32,256]{3,2,1,0:T(8,128)}, u32[]{:S(2)}) %copy-start) | copy-done | bytes 1572888
  2.0 0.0 copy-start.1
  2.0 0.8 %copy-done.1 = s32[32,256]{1,0:T(8,128)S(1)} copy-done((s32[32,256]{1,0:T(8,128)S(1)}, s32[32,256]{1,0:T(8,128)}, u32[]{:S(2)}) %copy-start.1) | copy-done | bytes 32792
  2.8 0.0 copy-start.3
  2.8 0.8 %copy-done.3 = f32[32,256]{1,0:T(8,128)S(1)} copy-done((f32[32,256]{1,0:T(8,128)S(1)}, f32[32,256]{1,0:T(8,128)}, u32[]{:S(2)}) %copy-start.3) | copy-done | bytes 32792
  3.6 0.1 shard_map.50
  3.6 2.2 %collective-permute-start = (f32[34,8,256]{2,1,0:T(8,128)S(1)}, f32[34,8,256]{2,1,0:T(8,128)S(1)}, u32[]{:S(2)}, u32[]{:S(2)}) collective-permute-start(f32[34,8,256]{2,1,0:T(8,128)S(1)} %get-tuple-element.13), channel_id=1, source_target_pairs={{0,1},{1,0},{2,3},{3,2},{4,5},{5,4},{6,7},{7,6},{8,9},{9,8},{10,11... | collective-permute-start | bytes 835592 | tf_op jit(solution)/shard_map/ppermute | solution.py:437
  5.8 0.7 %collective-permute-start.1 = (f32[34,8,256]{2,1,0:T(8,128)S(1)}, f32[34,8,256]{2,1,0:T(8,128)S(1)}, u32[]{:S(2)}, u32[]{:S(2)}) collective-permute-start(f32[34,8,256]{2,1,0:T(8,128)S(1)} %get-tuple-element.14), channel_id=1, source_target_pairs={{1,2},{2,1},{3,4},{4,3},{5,6},{6,5},{7,8},{8,7},{9,10},{10,9},{11,... | collective-permute-start | bytes 835592 | tf_op jit(solution)/shard_map/ppermute | solution.py:437
  6.5 4.5 %collective-permute-done.rows_even = f32[34,8,256]{2,1,0:T(8,128)S(1)} collective-permute-done((f32[34,8,256]{2,1,0:T(8,128)S(1)}, f32[34,8,256]{2,1,0:T(8,128)S(1)}, u32[]{:S(2)}, u32[]{:S(2)}) %collective-permute-start) | collective-permute-done | bytes 278560 | tf_op jit(solution)/shard_map/ppermute | solution.py:437
  11.0 0.0 collective-permute-done.1.rows_odd
  11.0 1.6 %shard_map.51 = (f32[4,48,128]{2,1,0:T(8,128)S(1)}, f32[4,48,128]{2,1,0:T(8,128)S(1)}) custom-call(f32[3,16,32,256]{3,2,1,0:T(8,128)S(1)} %copy-done, f32[3,16,32,256]{3,2,1,0:T(8,128)S(1)} %copy-done, s32[32,256]{1,0:T(8,128)S(1)} %copy-done.1, f32[32,256]{1,0:T(8,128)S(1)} %copy-done.3, f32[34,8,256]{2,1,0:T(8,128)S(1)} %collective-permute-done.rows_even, ...), custom_call_target="tpu_custom_call" | custom-call | tf_op jit(solution)/shard_map/pallas_call | solution.py:465
  12.6 0.0 copy-start.2
  12.6 0.0 copy-start.4
  12.6 2.6 %collective-permute-start.2 = (f32[4,48,128]{2,1,0:T(8,128)S(1)}, f32[4,48,128]{2,1,0:T(8,128)S(1)}, u32[]{:S(2)}, u32[]{:S(2)}) collective-permute-start(f32[4,48,128]{2,1,0:T(8,128)S(1)} %get-tuple-element.15.sent_even), channel_id=1, source_target_pairs={{0,16},{16,0},{32,48},{48,32},{64,80},{80,64},{96,112},{112,96},{1... | collective-permute-start | bytes 294920 | tf_op jit(solution)/shard_map/ppermute | solution.py:437
  15.2 1.7 %collective-permute-start.3 = (f32[4,48,128]{2,1,0:T(8,128)S(1)}, f32[4,48,128]{2,1,0:T(8,128)S(1)}, u32[]{:S(2)}, u32[]{:S(2)}) collective-permute-start(f32[4,48,128]{2,1,0:T(8,128)S(1)} %get-tuple-element.16.sent_odd), channel_id=1, source_target_pairs={{16,32},{32,16},{48,64},{64,48},{80,96},{96,80},{112,128},{128,112... | collective-permute-start | bytes 294920 | tf_op jit(solution)/shard_map/ppermute | solution.py:437
  17.0 3.1 %shard_map.52 = (f32[3,16,32,256]{3,2,1,0:T(8,128)S(1)}, f32[48,256]{1,0:T(8,128)S(1)}, f32[48,256]{1,0:T(8,128)S(1)}, f32[48,128]{1,0:T(8,128)S(1)}) custom-call(f32[3,16,32,256]{3,2,1,0:T(8,128)S(1)} %copy-done, s32[32,256]{1,0:T(8,128)S(1)} %copy-done.1, f32[34,8,256]{2,1,0:T(8,128)S(1)} %collective-permute-done.rows_even, ...), custom_call_target="tpu_custom_call" | custom-call | flops 23592960 | bytes 3145728 | tf_op jit(solution)/shard_map/pallas_call | solution.py:475
  20.1 0.0 collective-permute-done.2.got_even
  20.1 0.0 collective-permute-done.3.got_odd
  20.1 0.0 copy-done.2
  20.1 0.0 copy-done.4
  20.1 1.7 %shard_map.53 = (f32[2,3,32,128]{3,2,1,0:T(8,128)S(1)}, f32[5,48,384]{2,1,0:T(8,128)S(1)}, f32[1,128]{1,0:T(1,128)S(1)}) custom-call(f32[4,48,128]{2,1,0:T(8,128)S(1)} %get-tuple-element.15.sent_even, f32[4,48,128]{2,1,0:T(8,128)S(1)} %get-tuple-element.16.sent_odd, f32[4,48,128]{2,1,0:T(8,128)S(1)} %collective-permute-done.2.got_even, ...), custom_call_target="tpu_custom_call" | custom-call | tf_op jit(solution)/shard_map/pallas_call | solution.py:489
  21.8 0.1 broadcast_in_dim.9
  21.9 31.9 %all_to_all.5 = f32[256,1,128]{2,1,0:T(1,128)S(1)} all-to-all(f32[256,1,128]{2,1,0:T(1,128)S(1)} %broadcast_in_dim.9), channel_id=1, replica_groups=mesh['lon'=16,'lat'=16] {'lon','lat'}, dimensions={0} | all-to-all | bytes 262144 | tf_op jit(solution)/shard_map/all_to_all | solution.py:504
  53.8 3.5 %shard_map.54 = (f32[3,16,32,256]{3,2,1,0:T(8,128)}, f32[32,256]{1,0:T(8,128)}) custom-call(f32[256,128]{1,0:T(8,128)S(1)} %bitcast.2, f32[5,48,384]{2,1,0:T(8,128)S(1)} %get-tuple-element.21.basis, f32[2,3,32,128]{3,2,1,0:T(8,128)S(1)} %get-tuple-element.22.edges, s32[32,256]{1,0:T(8,128)S(1)} %copy-done.2, f32[3,16,32,256]{3,2,1,0:T(8,128)S(1)} %get-tuple-element.23.advanced), custom_call_target="tpu_custom_call" | custom-call | tf_op jit(solution)/shard_map/pallas_call | solution.py:505
Async XLA Ops:
  0.6 1.4 %copy-start = (f32[3,16,32,256]{3,2,1,0:T(8,128)S(1)}, f32[3,16,32,256]{3,2,1,0:T(8,128)}, u32[]{:S(2)}) copy-start(f32[3,16,32,256]{3,2,1,0:T(8,128)} %state.1) | copy-start | bytes 4718596
  2.0 0.8 %copy-start.1 = (s32[32,256]{1,0:T(8,128)S(1)}, s32[32,256]{1,0:T(8,128)}, u32[]{:S(2)}) copy-start(s32[32,256]{1,0:T(8,128)} %kmt.7) | copy-start | bytes 98308
  2.8 0.8 %copy-start.3 = (f32[32,256]{1,0:T(8,128)S(1)}, f32[32,256]{1,0:T(8,128)}, u32[]{:S(2)}) copy-start(f32[32,256]{1,0:T(8,128)} %guess.3) | copy-start | bytes 98308
  3.6 7.3 %collective-permute-start = (f32[34,8,256]{2,1,0:T(8,128)S(1)}, f32[34,8,256]{2,1,0:T(8,128)S(1)}, u32[]{:S(2)}, u32[]{:S(2)}) collective-permute-start(f32[34,8,256]{2,1,0:T(8,128)S(1)} %get-tuple-element.13), channel_id=1, source_target_pairs={{0,1},{1,0},{2,3},{3,2},{4,5},{5,4},{6,7},{7,6},{8,9},{9,8},{10,11... | collective-permute-start | bytes 835592 | tf_op jit(solution)/shard_map/ppermute | solution.py:437
  5.8 5.1 %collective-permute-start.1 = (f32[34,8,256]{2,1,0:T(8,128)S(1)}, f32[34,8,256]{2,1,0:T(8,128)S(1)}, u32[]{:S(2)}, u32[]{:S(2)}) collective-permute-start(f32[34,8,256]{2,1,0:T(8,128)S(1)} %get-tuple-element.14), channel_id=1, source_target_pairs={{1,2},{2,1},{3,4},{4,3},{5,6},{6,5},{7,8},{8,7},{9,10},{10,9},{11,... | collective-permute-start | bytes 835592 | tf_op jit(solution)/shard_map/ppermute | solution.py:437
  12.6 7.5 %copy-start.2 = (s32[32,256]{1,0:T(8,128)S(1)}, s32[32,256]{1,0:T(8,128)}, u32[]{:S(2)}) copy-start(s32[32,256]{1,0:T(8,128)} %kmt.7) | copy-start | bytes 98308
  12.6 7.5 %copy-start.4 = (f32[32,256]{1,0:T(8,128)S(1)}, f32[32,256]{1,0:T(8,128)}, u32[]{:S(2)}) copy-start(f32[32,256]{1,0:T(8,128)} %guess.3) | copy-start | bytes 98308
  12.6 7.4 %collective-permute-start.2 = (f32[4,48,128]{2,1,0:T(8,128)S(1)}, f32[4,48,128]{2,1,0:T(8,128)S(1)}, u32[]{:S(2)}, u32[]{:S(2)}) collective-permute-start(f32[4,48,128]{2,1,0:T(8,128)S(1)} %get-tuple-element.15.sent_even), channel_id=1, source_target_pairs={{0,16},{16,0},{32,48},{48,32},{64,80},{80,64},{96,112},{112,96},{1... | collective-permute-start | bytes 294920 | tf_op jit(solution)/shard_map/ppermute | solution.py:437
  15.2 4.8 %collective-permute-start.3 = (f32[4,48,128]{2,1,0:T(8,128)S(1)}, f32[4,48,128]{2,1,0:T(8,128)S(1)}, u32[]{:S(2)}, u32[]{:S(2)}) collective-permute-start(f32[4,48,128]{2,1,0:T(8,128)S(1)} %get-tuple-element.16.sent_odd), channel_id=1, source_target_pairs={{16,32},{32,16},{48,64},{64,48},{80,96},{96,80},{112,128},{128,112... | collective-permute-start | bytes 294920 | tf_op jit(solution)/shard_map/ppermute | solution.py:437
